TPU v7x, 1024 devices: a whole 4x8x16 slice. The times are simulated.
1024 devices in a mesh: dp: 4 (over x_hi, core), expert: 32 (over x_lo, z), tensor: 8 (over y).
Axes of the slice: x: 4 (x_hi: 2, x_lo: 2; x = x_hi * 2 + x_lo), y: 8, z: 16, core: 2. Of those that a mesh axis runs over, the one named last changes fastest.
Arguments:
- expert_partials: bfloat16 [4, 28672, 2048], P('dp', 'expert', 'tensor'), may hold values from -4096 to 4096
- token_counts: int32 [4, 4], P('dp'), may hold values from 256 to 2047
- expert_master: float32 [28672, 2048], P(('expert', 'dp'), 'tensor'), may hold values from -0.12 to 0.12
- expert_moment: float32 [28672, 2048], P(('expert', 'dp'), 'tensor'), may hold values from -6 to 6
- expert_second: float32 [28672, 2048], P(('expert', 'dp'), 'tensor'), may hold values from 0.01 to 4
- dense_partials: bfloat16 [128, 128, 8, 1024], P(('dp', 'expert'), None, 'tensor'), may hold values from -7 to 7
- dense_master: float32 [1048576], P(('dp', 'expert', 'tensor')), may hold values from -0.12 to 0.12
- dense_moment: float32 [1048576], P(('dp', 'expert', 'tensor')), may hold values from -6 to 6
- dense_second: float32 [1048576], P(('dp', 'expert', 'tensor')), may hold values from 0.01 to 4
Outputs:
- expert_weight: bfloat16 [28672, 2048], P('expert', 'tensor')
- expert_master_new: float32 [28672, 2048], P(('expert', 'dp'), 'tensor')
- expert_moment_new: float32 [28672, 2048], P(('expert', 'dp'), 'tensor')
- expert_second_new: float32 [28672, 2048], P(('expert', 'dp'), 'tensor')
- dense_weight: bfloat16 [128, 8, 1024], P(None, 'tensor')
- dense_master_new: float32 [1048576], P(('dp', 'expert', 'tensor'))
- dense_moment_new: float32 [1048576], P(('dp', 'expert', 'tensor'))
- dense_second_new: float32 [1048576], P(('dp', 'expert', 'tensor'))
Inputs may be any that keep to these rules, and one draw needn't show every extreme that they name: token_counts[r, e] is the number of tokens of data replica r routed to expert e.
All inputs are finite; a program needn't handle non-finite values.
Results may differ from a plain program's by a relative error of at most 0.014.
Values may be sent and summed in bfloat16 or wider, within the bound.
A program may use at most 32 MiB of HBM per device.

v0:
```python
import jax
import jax.numpy as jnp
from jax import lax
from jax.sharding import PartitionSpec as P

D = 7168


beta_one = 0.9
beta_two = 0.95
epsilon = 1e-08
learn_rate = 0.001
weight_decay = 0.1
bias_one = 1.0 - 0.9**10
bias_two = 1.0 - 0.95**10


def adam_update(weight, moment, second, gradient):
    moment_new = beta_one * moment + (1.0 - beta_one) * gradient
    second_new = beta_two * second + (1.0 - beta_two) * gradient * gradient
    ratio = moment_new / bias_one / (jnp.sqrt(second_new / bias_two) + epsilon)
    weight_new = weight - learn_rate * (ratio + weight_decay * weight)
    return (weight_new, moment_new, second_new)


def shards(
    expert_partials,
    token_counts,
    expert_master,
    expert_moment,
    expert_second,
    dense_partials,
    dense_master,
    dense_moment,
    dense_second,
):
    local_rows = expert_partials[0]
    row_total = local_rows.shape[0]
    first_row = lax.axis_index("expert") * row_total
    row_expert = (first_row + lax.broadcasted_iota(jnp.int32, (row_total, 1), 0)) // D
    counts = token_counts[0].astype(jnp.float32)
    matches = row_expert == lax.broadcasted_iota(jnp.int32, (1, counts.shape[0]), 1)
    row_count = jnp.sum(jnp.where(matches, counts[None, :], 0.0), axis=1, keepdims=True)
    scaled = local_rows.astype(jnp.float32) / row_count
    gradient = lax.psum_scatter(
        scaled.astype(jnp.bfloat16), "dp", scatter_dimension=0, tiled=True
    ).astype(jnp.float32)
    dense_part = dense_partials[0, :, 0, :].astype(jnp.float32)
    dense_gradient = lax.psum_scatter(dense_part, ("dp", "expert"), scatter_dimension=0, tiled=True)
    dense_gradient = dense_gradient.reshape(dense_master.shape[0])
    master_new, moment_new, second_new = adam_update(
        expert_master, expert_moment, expert_second, gradient
    )
    expert_weight = lax.all_gather(master_new.astype(jnp.bfloat16), "dp", axis=0, tiled=True)
    dense_new, dense_moment_new, dense_second_new = adam_update(
        dense_master, dense_moment, dense_second, dense_gradient
    )
    dense_shard = dense_new.astype(jnp.bfloat16).reshape(1, 1, dense_new.shape[0])
    dense_weight = lax.all_gather(dense_shard, ("dp", "expert"), axis=0, tiled=True)
    return (
        expert_weight,
        master_new,
        moment_new,
        second_new,
        dense_weight,
        dense_new,
        dense_moment_new,
        dense_second_new,
    )


def solution(mesh):
    return jax.shard_map(
        shards,
        mesh=mesh,
        in_specs=(
            P("dp", "expert", "tensor"),
            P("dp", None),
            P(("expert", "dp"), "tensor"),
            P(("expert", "dp"), "tensor"),
            P(("expert", "dp"), "tensor"),
            P(("dp", "expert"), None, "tensor", None),
            P(("dp", "expert", "tensor")),
            P(("dp", "expert", "tensor")),
            P(("dp", "expert", "tensor")),
        ),
        out_specs=(
            P("expert", "tensor"),
            P(("expert", "dp"), "tensor"),
            P(("expert", "dp"), "tensor"),
            P(("expert", "dp"), "tensor"),
            P(None, "tensor", None),
            P(("dp", "expert", "tensor")),
            P(("dp", "expert", "tensor")),
            P(("dp", "expert", "tensor")),
        ),
        check_vma=False,
    )
```

profile of v0, /device:TPU:1, one launch (start us, length us, event | category | flops | bytes accessed | tf_op | source)
XLA Modules:
  0.0 632.5 jit_solution(4737115915202298501)
XLA Ops:
  8.0 0.0 all-reduce.3.cloned.1.call-start
  8.0 1.8 bitcast_convert_fusion
  9.8 0.0 copy-start
  9.8 0.0 all-reduce.3.cloned.1.call-update
  9.9 0.0 reduce-scatter.2.cloned.1.call-start
  9.9 0.0 copy-start.7
  9.9 0.7 copy-done.7
  10.6 0.1 select_reduce_fusion
  10.7 0.1 copy-done
  10.9 1.0 fusion
  11.8 0.0 reduce-scatter.2.cloned.1.call-update
  11.9 1.3 dynamic-slice
  13.1 352.2 %all-reduce.3.cloned.1.call-done = f32[128,1024]{1,0:T(8,128)} async-done(((f32[128,1024]{1,0:T(8,128)}), f32[128,1024]{1,0:T(8,128)}) %all-reduce.3.cloned.1.call-update) | async-done | bytes 524304
  365.4 0.0 copy-start.6
  365.4 0.0 copy-start.4
  365.4 0.0 copy-start.5
  365.4 1.5 constant_dynamic-slice_fusion
  366.8 0.0 copy-done.6
  366.8 0.0 copy-done.4
  366.8 0.0 copy-done.5
  366.8 0.6 fusion.5
  367.5 0.0 copy-start.3
  367.5 221.2 %all-gather = bf16[131072]{0:T(1024)(128)(2,1)S(1)} all-gather(bf16[1024]{0:T(1024)(128)(2,1)S(1)} %get-tuple-element.8), channel_id=2, replica_groups=mesh['dp'=4,'expert'=32,'tensor'=8] {'dp','expert'}, dimensions={0}, use_global_device_ids=true | all-gather | bytes 264192 | tf_op jit(solution)/shard_map/all_gather | solution.py:59
  588.6 0.0 copy-start.1
  588.6 0.0 copy-start.2
  588.6 0.8 reshape.52
  589.5 0.0 reduce-scatter.2.cloned.1.call-done
  589.5 0.0 copy-done.3
  589.5 0.1 copy-done.1
  589.6 0.2 copy-done.2
  589.8 1.8 fusion.7
  591.6 32.7 %all_gather.6 = bf16[896,256]{1,0:T(8,128)(2,1)S(1)} all-gather(bf16[224,256]{1,0:T(8,128)(2,1)S(1)} %get-tuple-element.12), channel_id=1, replica_groups=mesh['dp'=4,'expert'=32,'tensor'=8] {'dp'}, dimensions={0}, use_global_device_ids=true | all-gather | bytes 573440 | tf_op jit(solution)/shard_map/all_gather | solution.py:54
  624.3 0.8 copy.19
  (2 shorter events, 0.0 us)
Async XLA Ops:
  8.0 357.4 %all-reduce.3.cloned.1.call-start = ((), (), s32[]{:S(2)}) async-start(), calls=%async_computation.2 | async-start | bytes 1048576
  9.8 1.0 copy-start
  9.9 579.6 %reduce-scatter.2.cloned.1.call-start = ((), (), s32[]{:S(2)}) async-start(), calls=%async_computation.1 | async-start | bytes 573440 | tf_op jit(solution)/shard_map/reduce_scatter | solution.py:45
  9.9 0.7 copy-start.7
  365.4 1.5 copy-start.6
  365.4 1.5 copy-start.4
  365.4 1.5 copy-start.5
  367.5 222.0 %copy-start.3 = (f32[224,256]{1,0:T(8,128)S(1)}, f32[224,256]{1,0:T(8,128)}, u32[]{:S(2)}) copy-start(f32[224,256]{1,0:T(8,128)} %param.13) | copy-start | bytes 688132
  588.6 0.9 copy-start.1
  588.6 1.1 copy-start.2
Sparse Core Ops, SparseCore 0:
  12.3 353.0 all-reduce.2
Sparse Core Ops, SparseCore 1:
  14.5 58.1 reduce-scatter.1
where the time goes:
time: 633 us
  waiting for transfers between devices  352 us (56%)
  blocking collectives  254 us (40%)
  between operations  15.5 us (2%)
    unnamed x3, waiting for transfers between devices  352 us
    all_gather x1, blocking collectives, shards(): lax.all_gather(dense_shard, ('dp', 'expert'), axis=0, tiled=True)  221 us
    all_gather x1, blocking collectives, shards(): lax.all_gather(master_new.astype(jnp.bfloat16), 'dp', axis=0, tiled=True)  32.7 us
  transfers between devices with their start and end apart: 2, of which 1 were waited for; matrix products, arithmetic and copies ran while one was open for 1% of the time, Pallas kernels for 0%

commit v1 on v0

v1 whole, which is shorter than its diff:
```python
import functools

import jax
import jax.numpy as jnp
from jax import lax
from jax.experimental import pallas as pl
from jax.experimental.pallas import tpu as pltpu
from jax.sharding import PartitionSpec as P

MESH = pl.DeviceIdType.MESH
F32 = jnp.float32
BF16 = jnp.bfloat16

beta_one = 0.9
beta_two = 0.95
epsilon = 1e-08
learn_rate = 0.001
weight_decay = 0.1
bias_one = 1.0 - 0.9**10
bias_two = 1.0 - 0.95**10

NX, NZ, NP = 4, 16, 4
NB = NZ // NP
ROWS = 224
COLS = 256
PER_EXPERT = 8
PIECE = NB * 8
NEAR = [(dx, dq) for dx in (2, 1, 3, 0) for dq in (2, 1, 3, 0) if (dx, dq) != (0, 0)]


def adam_update(weight, moment, second, gradient):
    moment_new = beta_one * moment + (1.0 - beta_one) * gradient
    second_new = beta_two * second + (1.0 - beta_two) * gradient * gradient
    ratio = moment_new / bias_one / (jnp.sqrt(second_new / bias_two) + epsilon)
    weight_new = weight - learn_rate * (ratio + weight_decay * weight)
    return (weight_new, moment_new, second_new)


def at(offset, size, unit):
    return pl.ds(pl.multiple_of(offset, unit), size)


def exchange(
    partials, counts, master, moment, second, dense, dmaster, dmoment, dsecond,
    weight_out, master_out, moment_out, second_out, dweight_out, dmaster_out, dmoment_out, dsecond_out,
    counts_s, blocks, states, scaled, pair_in, cross_send, cross_in,
    dense_own, dense_in, tiles, pieces, near_in, far_buf, dstates, dnew, dweights, spread,
    load_sem, pair_send, pair_recv, near_send, near_recv, far_send, far_recv,
    cross_ss, cross_rs, gather_send, gather_recv, back_send, back_recv, known,
):
    dp, ex = lax.axis_index("dp"), lax.axis_index("expert")
    xh, c = dp // 2, dp % 2
    xl, z = ex // NZ, ex % NZ
    x = 2 * xh + xl
    zb, q = z // NP, z % NP
    mine = x * NP + q

    def device(x, z, c):
        return {"dp": (x // 2) * 2 + c, "expert": (x % 2) * NZ + z}

    pair = device(x, z, 1 - c)
    cross = device((x + 2) % NX, z, c)
    near = [device((x + dx) % NX, zb * NP + (q + dq) % NP, c) for dx, dq in NEAR]
    far = [device(x, (z + NP * d) % NZ, c) for d in range(1, NB)]

    def send(src, dst, ss, rs, to):
        return pltpu.make_async_remote_copy(
            src_ref=src, dst_ref=dst, send_sem=ss, recv_sem=rs, device_id=to, device_id_type=MESH
        )

    def block(index, slot, sem):
        return pltpu.make_async_copy(
            partials.at[at(index * ROWS, ROWS, 32)], blocks.at[pl.ds(slot * ROWS, ROWS)], load_sem.at[sem]
        )

    load_counts = pltpu.make_async_copy(counts, counts_s, load_sem.at[0])
    load_blocks = [
        block(2 * xh + 1 - c, 0, 1),
        block(2 * (1 - xh) + 1 - c, 1, 2),
        block(2 * (1 - xh) + c, 2, 3),
        block(2 * xh + c, 3, 4),
    ]
    load_dense = [
        pltpu.make_async_copy(
            dense.at[at((2 * h + c) * 32, 32, 32)], dense_own.at[pl.ds(h * 32, 32)], load_sem.at[5 + h]
        )
        for h in range(2)
    ]
    load_dstates = [
        pltpu.make_async_copy(ref, dstates.at[at(zb * 24 + 8 * i, 8, 8)], load_sem.at[7 + i])
        for i, ref in enumerate((dmaster, dmoment, dsecond))
    ]
    load_states = [
        pltpu.make_async_copy(ref, states.at[i], load_sem.at[10 + i])
        for i, ref in enumerate((master, moment, second))
    ]
    load_counts.start()
    for copy in load_dense + load_blocks + load_dstates + load_states:
        copy.start()

    barrier = pltpu.get_barrier_semaphore()
    greeted = [pair] + near + [far[0], far[-1]]
    for other in greeted:
        pl.semaphore_signal(barrier, inc=1, device_id=other, device_id_type=MESH)

    load_counts.wait()
    count = counts_s[0, ex // PER_EXPERT].astype(F32)
    inverse = 1.0 / jnp.full((1, COLS), count, F32)

    def scale(slot, start):
        rows = blocks[pl.ds(slot * ROWS + start, 32)].astype(F32) * inverse
        return rows.astype(BF16)

    load_blocks[0].wait()
    load_blocks[1].wait()

    def scale_step(i, carry):
        rows = pl.ds(pl.multiple_of(i * 32, 32), 32)
        scaled[rows] = (blocks[rows].astype(F32) * inverse).astype(BF16)
        return carry

    lax.fori_loop(0, 2 * ROWS // 32, scale_step, 0)

    pl.semaphore_wait(barrier, len(greeted))

    dense_pair = [
        send(
            dense.at[at((2 * h + 1 - c) * 32, 32, 32)], dense_in.at[pl.ds(h * 32, 32)],
            pair_send.at[h], pair_recv.at[h], pair,
        )
        for h in range(2)
    ]
    block_pair = [
        send(
            scaled.at[pl.ds(h * ROWS, ROWS)], pair_in.at[pl.ds(h * ROWS, ROWS)],
            pair_send.at[2 + h], pair_recv.at[2 + h], pair,
        )
        for h in range(2)
    ]
    for copy in dense_pair + block_pair[::-1]:
        copy.start()
    pl.semaphore_signal(known, inc=1, device_id=far[0], device_id_type=MESH)

    for copy in load_dense:
        copy.wait()
    for copy in dense_pair:
        copy.wait_recv()
    for xx in range(NX):
        rows = pl.ds(xx * NZ, NZ)
        total = dense_own[rows].astype(F32) + dense_in[rows].astype(F32)
        for s in range(8):
            tiles[pl.ds(xx * NZ * 8 + s, NZ, stride=8), :] = total[:, s * 128 : (s + 1) * 128]
    for xx in range(NX):
        for qq in range(NP):
            t = xx * NP + qq
            for half in range(NB // 2):
                two = [tiles[pl.ds((xx * NZ + NP * (2 * half + k) + qq) * 8, 8), :] for k in range(2)]
                pieces[pl.ds(t * PIECE + half * 16, 16), :] = jnp.concatenate(two, axis=0).astype(BF16)

    to_near = []
    for k, (dx, dq) in enumerate(NEAR):
        t = ((x + dx) % NX) * NP + (q + dq) % NP
        copy = send(
            pieces.at[at(t * PIECE, PIECE, 32)], near_in.at[pl.ds(k * PIECE, PIECE)],
            near_send.at[k], near_recv.at[k], near[k],
        )
        copy.start()
        to_near.append(copy)

    load_blocks[2].wait()
    block_pair[1].wait_recv()

    def cross_step(i, carry):
        off = pl.multiple_of(i * 32, 32)
        own = (blocks[pl.ds(pl.multiple_of(2 * ROWS + off, 32), 32)].astype(F32) * inverse).astype(BF16)
        other = pair_in[pl.ds(pl.multiple_of(ROWS + off, 32), 32)]
        cross_send[pl.ds(off, 32)] = (own.astype(F32) + other.astype(F32)).astype(BF16)
        return carry

    lax.fori_loop(0, ROWS // 32, cross_step, 0)
    to_cross = send(cross_send, cross_in, cross_ss.at[0], cross_rs.at[0], cross)
    to_cross.start()

    for copy in load_dstates:
        copy.wait()
    pl.semaphore_wait(known, 1)
    own_states = dstates.at[at(zb * 24, 24, 8)]
    to_states = [
        send(own_states, own_states, far_send.at[d], far_recv.at[d], far[d]) for d in range(NB - 1)
    ]
    for copy in to_states:
        copy.start()

    total = [tiles[at((x * NZ + NP * b + q) * 8, 8, 8), :] for b in range(NB)]
    total = jnp.concatenate(total, axis=0)
    for k, copy in enumerate(to_near):
        copy.wait_recv()
        total = total + near_in[pl.ds(k * PIECE, PIECE), :].astype(F32)
    far_own = far_buf.at[at(zb * PIECE, PIECE, 32)]
    far_own[...] = total.astype(BF16)
    to_far = [
        send(far_own, far_own, far_send.at[NB - 1 + d], far_recv.at[NB - 1 + d], far[d])
        for d in (1, 0, 2)
    ]
    for copy in to_far:
        copy.start()

    load_blocks[3].wait()
    block_pair[0].wait_recv()
    for copy in load_states:
        copy.wait()
    to_cross.wait_recv()

    def update_step(i, carry):
        off = pl.multiple_of(i * 32, 32)
        rows = pl.ds(off, 32)
        own = (blocks[pl.ds(pl.multiple_of(3 * ROWS + off, 32), 32)].astype(F32) * inverse).astype(BF16)
        gradient = own.astype(F32) + pair_in[rows].astype(F32) + cross_in[rows].astype(F32)
        new, moment_new, second_new = adam_update(states[0, rows], states[1, rows], states[2, rows], gradient)
        master_out[rows] = new
        moment_out[rows] = moment_new
        second_out[rows] = second_new
        weight_out[pl.ds(pl.multiple_of(dp * ROWS + off, 32), 32)] = new.astype(BF16)
        return carry

    lax.fori_loop(0, ROWS // 32, update_step, 0)
    own_weight = weight_out.at[at(dp * ROWS, ROWS, 32)]
    weight_cross = send(own_weight, own_weight, cross_ss.at[1], cross_rs.at[1], cross)
    weight_cross.start()
    weight_pair = send(own_weight, own_weight, cross_ss.at[2], cross_rs.at[2], pair)
    weight_pair.start()

    for copy in to_states + to_far:
        copy.wait_recv()
    dense_sum = jnp.zeros((PIECE, 128), F32)
    for b in range(NB):
        dense_sum = dense_sum + far_buf[pl.ds(b * PIECE, PIECE), :].astype(F32)
    news = []
    for b in range(NB):
        old = [dstates[pl.ds(b * 24 + 8 * i, 8), :] for i in range(3)]
        new = adam_update(*old, dense_sum[b * 8 : (b + 1) * 8])
        for i in range(3):
            dnew[pl.ds(b * 24 + 8 * i, 8), :] = new[i]
        news.append(new[0])
    own_piece = dweights.at[at(c * 512 + mine * PIECE, PIECE, 32)]
    own_piece[...] = jnp.concatenate(news, axis=0).astype(BF16)
    to_gather = [send(own_piece, own_piece, gather_send.at[k], gather_recv.at[k], near[k]) for k in range(len(NEAR))]
    for copy in to_gather:
        copy.start()
    for i, ref in enumerate((dmaster_out, dmoment_out, dsecond_out)):
        ref[...] = dnew[at(zb * 24 + 8 * i, 8, 8), :]

    weight_cross.wait_recv()
    cross_weight = weight_out.at[at((2 * (1 - xh) + c) * ROWS, ROWS, 32)]
    weight_on = send(cross_weight, cross_weight, cross_ss.at[3], cross_rs.at[3], pair)
    weight_on.start()

    def place(core, xx):
        first = pl.multiple_of(core * 512 + xx * NP * PIECE, 128)
        for qq in range(NP):
            piece = dweights[pl.ds(pl.multiple_of(first + qq * PIECE, 32), PIECE), :].astype(F32)
            for b in range(NB):
                spread[pl.ds((NP * b + qq) * 8, 8), :] = piece[b * 8 : (b + 1) * 8]
        to = at(((xx // 2) * 2 + core) * 32 + (xx % 2) * NZ, NZ, 16)
        for s in range(8):
            dweight_out[to, s * 128 : (s + 1) * 128] = spread[pl.ds(s, NZ, stride=8), :].astype(BF16)

    backs = []
    for n, dx in enumerate((0, 1, 3, 2)):
        for k, (ddx, dq) in enumerate(NEAR):
            if ddx == dx:
                to_gather[k].wait_recv()
        group = dweights.at[at(c * 512 + ((x - dx) % NX) * NP * PIECE, NP * PIECE, 128)]
        back = send(group, group, back_send.at[n], back_recv.at[n], pair)
        back.start()
        backs.append(back)
        place(c, (x - dx) % NX)
    for n, dx in enumerate((0, 1, 3, 2)):
        backs[n].wait_recv()
        place(1 - c, (x - dx) % NX)

    weight_pair.wait_recv()
    weight_on.wait_recv()
    for copy in (
        dense_pair + block_pair + to_near + [to_cross] + to_states + to_far
        + [weight_cross, weight_pair, weight_on] + to_gather + backs
    ):
        copy.wait_send()


def store(*refs):
    sources, outs, sem = refs[:8], refs[8:16], refs[16]
    copies = [pltpu.make_async_copy(s, o, sem.at[i]) for i, (s, o) in enumerate(zip(sources, outs))]
    for copy in copies:
        copy.start()
    for copy in copies:
        copy.wait()


def shards(
    expert_partials,
    token_counts,
    expert_master,
    expert_moment,
    expert_second,
    dense_partials,
    dense_master,
    dense_moment,
    dense_second,
):
    hbm = pl.BlockSpec(memory_space=pltpu.HBM)
    vmem = pl.BlockSpec(memory_space=pltpu.VMEM)
    dma = pltpu.SemaphoreType.DMA
    shapes = [
        ((4 * ROWS, COLS), BF16),
        ((ROWS, COLS), F32),
        ((ROWS, COLS), F32),
        ((ROWS, COLS), F32),
        ((128, 1024), BF16),
        ((8, 128), F32),
        ((8, 128), F32),
        ((8, 128), F32),
    ]
    n = len(NEAR)
    results = pl.pallas_call(
        exchange,
        out_shape=[pltpu.VMEM(s, d) for s, d in shapes],
        in_specs=[hbm] * 9,
        out_specs=[vmem] * 8,
        scratch_shapes=[
            pltpu.SMEM((1, 4), jnp.int32),
            pltpu.VMEM((4 * ROWS, COLS), BF16),
            pltpu.VMEM((3, ROWS, COLS), F32),
            pltpu.VMEM((2 * ROWS, COLS), BF16),
            pltpu.VMEM((2 * ROWS, COLS), BF16),
            pltpu.VMEM((ROWS, COLS), BF16),
            pltpu.VMEM((ROWS, COLS), BF16),
            pltpu.VMEM((64, 1024), BF16),
            pltpu.VMEM((64, 1024), BF16),
            pltpu.VMEM((512, 128), F32),
            pltpu.VMEM((512, 128), BF16),
            pltpu.VMEM((n * PIECE, 128), BF16),
            pltpu.VMEM((NB * PIECE, 128), BF16),
            pltpu.VMEM((NB * 24, 128), F32),
            pltpu.VMEM((NB * 24, 128), F32),
            pltpu.VMEM((1024, 128), BF16),
            pltpu.VMEM((128, 128), F32),
            dma((13,)),
            dma((4,)),
            dma((4,)),
            dma((n,)),
            dma((n,)),
            dma((6,)),
            dma((6,)),
            dma((4,)),
            dma((4,)),
            dma((n,)),
            dma((n,)),
            dma((4,)),
            dma((4,)),
            pltpu.SemaphoreType.REGULAR,
        ],
        compiler_params=pltpu.CompilerParams(
            collective_id=0, has_side_effects=True, vmem_limit_bytes=24 * 2**20
        ),
        name="exchange",
    )(
        expert_partials.reshape(4 * ROWS, COLS),
        token_counts,
        expert_master,
        expert_moment,
        expert_second,
        dense_partials.reshape(128, 1024),
        dense_master.reshape(8, 128),
        dense_moment.reshape(8, 128),
        dense_second.reshape(8, 128),
    )
    outs = pl.pallas_call(
        store,
        out_shape=[jax.ShapeDtypeStruct(s, d) for s, d in shapes],
        in_specs=[vmem] * 8,
        out_specs=[hbm] * 8,
        scratch_shapes=[dma((8,))],
        compiler_params=pltpu.CompilerParams(vmem_limit_bytes=8 * 2**20),
        name="store",
    )(*results)
    outs = list(outs)
    outs[4] = outs[4].reshape(128, 1, 1024)
    for i in (5, 6, 7):
        outs[i] = outs[i].reshape(1024)
    return tuple(outs)


def solution(mesh):
    return jax.shard_map(
        shards,
        mesh=mesh,
        in_specs=(
            P("dp", "expert", "tensor"),
            P("dp", None),
            P(("expert", "dp"), "tensor"),
            P(("expert", "dp"), "tensor"),
            P(("expert", "dp"), "tensor"),
            P(("dp", "expert"), None, "tensor", None),
            P(("dp", "expert", "tensor")),
            P(("dp", "expert", "tensor")),
            P(("dp", "expert", "tensor")),
        ),
        out_specs=(
            P("expert", "tensor"),
            P(("expert", "dp"), "tensor"),
            P(("expert", "dp"), "tensor"),
            P(("expert", "dp"), "tensor"),
            P(None, "tensor", None),
            P(("dp", "expert", "tensor")),
            P(("dp", "expert", "tensor")),
            P(("dp", "expert", "tensor")),
        ),
        check_vma=False,
    )
```

time: 633 us -> 51.9 us (0.08)
  waiting for transfers between devices: 352 us -> 0 us
  blocking collectives: 254 us -> 0 us
  Pallas kernels: 0 us -> 44.7 us
  between operations: 15.5 us -> 0.68 us
    unnamed x3 -> x0, waiting for transfers between devices: 352 us -> none
    all_gather x2 -> x0, blocking collectives: 254 us -> none  [the longest x1 221 us: shards(): lax.all_gather(dense_shard, ('dp', 'expert'), axis=0, tiled=True)]
    pallas_call x0 -> x2, Pallas kernels: none -> 44.7 us  [the longest x1 43.6 us: shards(): pl.pallas_call(exchange, out_shape=[pltpu.VMEM(s, d) for s, d in shapes],...]
  transfers between devices with their start and end apart: 2 -> 0, of which waited for: 1 -> 0; matrix products, arithmetic and copies ran while one was open for 1% -> 0% of each run, Pallas kernels for 0% -> 0%
where the time goes in v1:
time: 51.9 us; the launch traced here: 51.5 us
  Pallas kernels  44.7 us (86%)
  local copies, waits for them, and re-layouts  6.15 us (12%)
  between operations  0.68 us (1%)
    pallas_call x1, Pallas kernels, shards(): pl.pallas_call(exchange, out_shape=[pltpu.VMEM(s, d) for s, d in shapes],...  43.6 us
    unnamed x18, local copies, waits for them, and re-layouts  6.15 us
    pallas_call x1, Pallas kernels, shards(): pl.pallas_call(store, out_shape=[jax.ShapeDtypeStruct(s, d) for s, d in s...  1.16 us

profile of v1, /device:TPU:1, one launch (start us, length us, event | category | flops | bytes accessed | tf_op | source)
XLA Modules:
  0.0 51.5 jit_solution(4682841449449991664)
XLA Ops:
  0.6 0.0 copy-start.6
  0.6 0.0 copy-start.5
  0.7 0.0 copy-start.8
  0.7 0.7 %copy-done.6 = f32[1024]{0:T(1024)S(1)} copy-done((f32[1024]{0:T(1024)S(1)}, f32[1024]{0:T(1024)}, u32[]{:S(2)}) %copy-start.6) | copy-done | bytes 4120
  1.3 0.0 copy-done.5
  1.3 0.0 copy-done.8
  1.3 0.0 copy-start
  1.3 1.0 %copy-done = bf16[1,896,256]{2,1,0:T(8,128)(2,1)S(1)} copy-done((bf16[1,896,256]{2,1,0:T(8,128)(2,1)S(1)}, bf16[1,896,256]{2,1,0:T(8,128)(2,1)}, u32[]{:S(2)}) %copy-start) | copy-done | bytes 458776
  2.4 0.0 copy-start.1
  2.4 0.9 %copy-done.1 = bf16[1,128,1,1024]{3,1,2,0:T(8,128)(2,1)S(1)} copy-done((bf16[1,128,1,1024]{3,1,2,0:T(8,128)(2,1)S(1)}, bf16[1,128,1,1024]{3,1,2,0:T(8,128)(2,1)}, u32[]{:S(2)}) %copy-start.1) | copy-done | bytes 262168
  3.3 0.0 copy-start.2
  3.3 0.9 %copy-done.2 = f32[224,256]{1,0:T(8,128)S(1)} copy-done((f32[224,256]{1,0:T(8,128)S(1)}, f32[224,256]{1,0:T(8,128)}, u32[]{:S(2)}) %copy-start.2) | copy-done | bytes 229400
  4.3 0.0 copy-start.3
  4.3 0.9 %copy-done.3 = f32[224,256]{1,0:T(8,128)S(1)} copy-done((f32[224,256]{1,0:T(8,128)S(1)}, f32[224,256]{1,0:T(8,128)}, u32[]{:S(2)}) %copy-start.3) | copy-done | bytes 229400
  5.2 0.0 copy-start.4
  5.2 0.9 %copy-done.4 = f32[224,256]{1,0:T(8,128)S(1)} copy-done((f32[224,256]{1,0:T(8,128)S(1)}, f32[224,256]{1,0:T(8,128)}, u32[]{:S(2)}) %copy-start.4) | copy-done | bytes 229400
  6.1 0.0 copy-start.7
  6.1 0.7 %copy-done.7 = f32[1024]{0:T(1024)S(1)} copy-done((f32[1024]{0:T(1024)S(1)}, f32[1024]{0:T(1024)}, u32[]{:S(2)}) %copy-start.7) | copy-done | bytes 4120
  6.8 43.6 %exchange.1 = (bf16[896,256]{1,0:T(8,128)(2,1)S(1)}, f32[224,256]{1,0:T(8,128)S(1)}, f32[224,256]{1,0:T(8,128)S(1)}, f32[224,256]{1,0:T(8,128)S(1)}, bf16[128,10...) custom-call(bf16[896,256]{1,0:T(8,128)(2,1)S(1)} %bitcast.9, ...), custom_call_target="tpu_custom_call" | custom-call | tf_op jit(solution)/shard_map/exchange/pallas_call | solution.py:325
  50.4 1.2 %store.1 = (bf16[896,256]{1,0:T(8,128)(2,1)}, f32[224,256]{1,0:T(8,128)}, f32[224,256]{1,0:T(8,128)}, f32[224,256]{1,0:T(8,128)}, bf16[128,1024]{1,0:T(8,128)(2,...) custom-call(bf16[896,256]{1,0:T(8,128)(2,1)S(1)} %get-tuple-element.24.refs_0_, ...), custom_call_target="tpu_custom_call" | custom-call | tf_op jit(solution)/shard_map/store/pallas_call | solution.py:378
Async XLA Ops:
  0.6 0.7 %copy-start.6 = (f32[1024]{0:T(1024)S(1)}, f32[1024]{0:T(1024)}, u32[]{:S(2)}) copy-start(f32[1024]{0:T(1024)} %param.16) | copy-start | bytes 12292
  0.6 0.7 %copy-start.5 = (f32[1024]{0:T(1024)S(1)}, f32[1024]{0:T(1024)}, u32[]{:S(2)}) copy-start(f32[1024]{0:T(1024)} %param.15) | copy-start | bytes 12292
  0.7 0.7 %copy-start.8 = (s32[1,4]{1,0:T(1,128)S(1)}, s32[1,4]{1,0:T(1,128)}, u32[]{:S(2)}) copy-start(s32[1,4]{1,0:T(1,128)} %counts.1) | copy-start | bytes 52
  1.3 1.0 %copy-start = (bf16[1,896,256]{2,1,0:T(8,128)(2,1)S(1)}, bf16[1,896,256]{2,1,0:T(8,128)(2,1)}, u32[]{:S(2)}) copy-start(bf16[1,896,256]{2,1,0:T(8,128)(2,1)} %param.9) | copy-start | bytes 1376260
  2.4 0.9 %copy-start.1 = (bf16[1,128,1,1024]{3,1,2,0:T(8,128)(2,1)S(1)}, bf16[1,128,1,1024]{3,1,2,0:T(8,128)(2,1)}, u32[]{:S(2)}) copy-start(bf16[1,128,1,1024]{3,1,2,0:T(8,128)(2,1)} %param.14) | copy-start | bytes 786436
  3.3 0.9 %copy-start.2 = (f32[224,256]{1,0:T(8,128)S(1)}, f32[224,256]{1,0:T(8,128)}, u32[]{:S(2)}) copy-start(f32[224,256]{1,0:T(8,128)} %master.1) | copy-start | bytes 688132
  4.3 0.9 %copy-start.3 = (f32[224,256]{1,0:T(8,128)S(1)}, f32[224,256]{1,0:T(8,128)}, u32[]{:S(2)}) copy-start(f32[224,256]{1,0:T(8,128)} %moment.1) | copy-start | bytes 688132
  5.2 0.9 %copy-start.4 = (f32[224,256]{1,0:T(8,128)S(1)}, f32[224,256]{1,0:T(8,128)}, u32[]{:S(2)}) copy-start(f32[224,256]{1,0:T(8,128)} %second.1) | copy-start | bytes 688132
  6.1 0.7 %copy-start.7 = (f32[1024]{0:T(1024)S(1)}, f32[1024]{0:T(1024)}, u32[]{:S(2)}) copy-start(f32[1024]{0:T(1024)} %param.17) | copy-start | bytes 12292

commit v2 on v1

--- a/solution.py
+++ b/solution.py
@@ -19,13 +19,15 @@
 bias_one = 1.0 - 0.9**10
 bias_two = 1.0 - 0.95**10
 
-NX, NZ, NP = 4, 16, 4
-NB = NZ // NP
+NX, NZ, NQ = 4, 16, 4
+NB = NZ // NQ
 ROWS = 224
 COLS = 256
 PER_EXPERT = 8
 PIECE = NB * 8
-NEAR = [(dx, dq) for dx in (2, 1, 3, 0) for dq in (2, 1, 3, 0) if (dx, dq) != (0, 0)]
+DX = (2, 1, 3, 0)
+DZ = (-2, 1, -1, 0)
+NEAR = [(dx, dz) for dx in DX for dz in DZ if (dx, dz) != (0, 0)]
 
 
 def adam_update(weight, moment, second, gradient):
@@ -52,21 +54,29 @@
     xh, c = dp // 2, dp % 2
     xl, z = ex // NZ, ex % NZ
     x = 2 * xh + xl
-    zb, q = z // NP, z % NP
-    mine = x * NP + q
+    zb, q = z // NQ, z % NQ
+    sign = 1 - 2 * c
+    columns = [(x + dx) % NX for dx in DX]
 
     def device(x, z, c):
-        return {"dp": (x // 2) * 2 + c, "expert": (x % 2) * NZ + z}
+        return {"dp": ((x % NX) // 2) * 2 + c, "expert": (x % 2) * NZ + z % NZ}
+
+    def along(dz):
+        return (z + sign * dz + NZ) % NZ
 
     pair = device(x, z, 1 - c)
-    cross = device((x + 2) % NX, z, c)
-    near = [device((x + dx) % NX, zb * NP + (q + dq) % NP, c) for dx, dq in NEAR]
-    far = [device(x, (z + NP * d) % NZ, c) for d in range(1, NB)]
+    cross = device(x + 2, z, c)
+    near = [device(x + dx, along(dz), c) for dx, dz in NEAR]
+    near_back = [device(x + NX - dx, along(-dz), c) for dx, dz in NEAR]
+    far = [device(x, z + NQ * d, c) for d in range(1, NB)]
 
     def send(src, dst, ss, rs, to):
         return pltpu.make_async_remote_copy(
             src_ref=src, dst_ref=dst, send_sem=ss, recv_sem=rs, device_id=to, device_id_type=MESH
         )
+
+    def dense_rows(column, core):
+        return at(((column // 2) * 2 + core) * 32 + (column % 2) * NZ, NZ, 16)
 
     def block(index, slot, sem):
         return pltpu.make_async_copy(
@@ -82,90 +92,93 @@
     ]
     load_dense = [
         pltpu.make_async_copy(
-            dense.at[at((2 * h + c) * 32, 32, 32)], dense_own.at[pl.ds(h * 32, 32)], load_sem.at[5 + h]
+            dense.at[dense_rows(column, c)], dense_own.at[pl.ds(n * NZ, NZ)], load_sem.at[5 + n]
         )
-        for h in range(2)
+        for n, column in enumerate(columns)
     ]
     load_dstates = [
-        pltpu.make_async_copy(ref, dstates.at[at(zb * 24 + 8 * i, 8, 8)], load_sem.at[7 + i])
+        pltpu.make_async_copy(ref, dstates.at[at(zb * 24 + 8 * i, 8, 8)], load_sem.at[9 + i])
         for i, ref in enumerate((dmaster, dmoment, dsecond))
     ]
     load_states = [
-        pltpu.make_async_copy(ref, states.at[i], load_sem.at[10 + i])
+        pltpu.make_async_copy(ref, states.at[i], load_sem.at[12 + i])
         for i, ref in enumerate((master, moment, second))
     ]
-    load_counts.start()
-    for copy in load_dense + load_blocks + load_dstates + load_states:
-        copy.start()
 
     barrier = pltpu.get_barrier_semaphore()
-    greeted = [pair] + near + [far[0], far[-1]]
+    greeted = near_back + [pair, far[0], far[-1]]
     for other in greeted:
         pl.semaphore_signal(barrier, inc=1, device_id=other, device_id_type=MESH)
+
+    load_counts.start()
+    for copy in load_blocks[:2] + load_dense + load_dstates + load_blocks[2:] + load_states:
+        copy.start()
 
     load_counts.wait()
     count = counts_s[0, ex // PER_EXPERT].astype(F32)
     inverse = 1.0 / jnp.full((1, COLS), count, F32)
-
-    def scale(slot, start):
-        rows = blocks[pl.ds(slot * ROWS + start, 32)].astype(F32) * inverse
-        return rows.astype(BF16)
-
     load_blocks[0].wait()
     load_blocks[1].wait()
 
     def scale_step(i, carry):
-        rows = pl.ds(pl.multiple_of(i * 32, 32), 32)
+        rows = pl.ds(pl.multiple_of(i * 64, 64), 64)
         scaled[rows] = (blocks[rows].astype(F32) * inverse).astype(BF16)
         return carry
 
-    lax.fori_loop(0, 2 * ROWS // 32, scale_step, 0)
-
-    pl.semaphore_wait(barrier, len(greeted))
+    lax.fori_loop(0, 2 * ROWS // 64, scale_step, 0)
+    for copy in load_dstates:
+        copy.wait()
+
+    pl.semaphore_wait(barrier, len(near) + 3)
 
     dense_pair = [
         send(
-            dense.at[at((2 * h + 1 - c) * 32, 32, 32)], dense_in.at[pl.ds(h * 32, 32)],
-            pair_send.at[h], pair_recv.at[h], pair,
+            dense.at[dense_rows(column, 1 - c)], dense_in.at[pl.ds(n * NZ, NZ)],
+            pair_send.at[n], pair_recv.at[n], pair,
         )
-        for h in range(2)
+        for n, column in enumerate(columns)
     ]
     block_pair = [
         send(
             scaled.at[pl.ds(h * ROWS, ROWS)], pair_in.at[pl.ds(h * ROWS, ROWS)],
-            pair_send.at[2 + h], pair_recv.at[2 + h], pair,
+            pair_send.at[4 + h], pair_recv.at[4 + h], pair,
         )
         for h in range(2)
     ]
     for copy in dense_pair + block_pair[::-1]:
         copy.start()
     pl.semaphore_signal(known, inc=1, device_id=far[0], device_id_type=MESH)
-
-    for copy in load_dense:
-        copy.wait()
-    for copy in dense_pair:
-        copy.wait_recv()
-    for xx in range(NX):
-        rows = pl.ds(xx * NZ, NZ)
+    own_states = dstates.at[at(zb * 24, 24, 8)]
+    to_states = [
+        send(own_states, own_states, far_send.at[d], far_recv.at[d], far[d]) for d in range(NB - 1)
+    ]
+    to_states[0].start()
+    to_states[2].start()
+
+    to_near = []
+    for n, dx in enumerate(DX):
+        load_dense[n].wait()
+        dense_pair[n].wait_recv()
+        rows = pl.ds(n * NZ, NZ)
         total = dense_own[rows].astype(F32) + dense_in[rows].astype(F32)
         for s in range(8):
-            tiles[pl.ds(xx * NZ * 8 + s, NZ, stride=8), :] = total[:, s * 128 : (s + 1) * 128]
-    for xx in range(NX):
-        for qq in range(NP):
-            t = xx * NP + qq
+            tiles[pl.ds(n * NZ * 8 + s, NZ, stride=8), :] = total[:, s * 128 : (s + 1) * 128]
+        for qq in range(NQ):
             for half in range(NB // 2):
-                two = [tiles[pl.ds((xx * NZ + NP * (2 * half + k) + qq) * 8, 8), :] for k in range(2)]
-                pieces[pl.ds(t * PIECE + half * 16, 16), :] = jnp.concatenate(two, axis=0).astype(BF16)
-
-    to_near = []
-    for k, (dx, dq) in enumerate(NEAR):
-        t = ((x + dx) % NX) * NP + (q + dq) % NP
-        copy = send(
-            pieces.at[at(t * PIECE, PIECE, 32)], near_in.at[pl.ds(k * PIECE, PIECE)],
-            near_send.at[k], near_recv.at[k], near[k],
-        )
-        copy.start()
-        to_near.append(copy)
+                two = [tiles[pl.ds((n * NZ + NQ * (2 * half + k) + qq) * 8, 8), :] for k in range(2)]
+                pieces[pl.ds((n * NQ + qq) * PIECE + half * 16, 16), :] = jnp.concatenate(two, axis=0).astype(BF16)
+        for k, (ddx, dz) in enumerate(NEAR):
+            if ddx == dx:
+                copy = send(
+                    pieces.at[at((n * NQ + along(dz) % NQ) * PIECE, PIECE, 32)],
+                    near_in.at[pl.ds(k * PIECE, PIECE)],
+                    near_send.at[k], near_recv.at[k], near[k],
+                )
+                copy.start()
+                to_near.append(copy)
+
+    pl.semaphore_wait(known, 1)
+    to_states[1].start()
 
     load_blocks[2].wait()
     block_pair[1].wait_recv()
@@ -179,22 +192,13 @@
 
     lax.fori_loop(0, ROWS // 32, cross_step, 0)
     to_cross = send(cross_send, cross_in, cross_ss.at[0], cross_rs.at[0], cross)
-    to_cross.start()
-
-    for copy in load_dstates:
-        copy.wait()
-    pl.semaphore_wait(known, 1)
-    own_states = dstates.at[at(zb * 24, 24, 8)]
-    to_states = [
-        send(own_states, own_states, far_send.at[d], far_recv.at[d], far[d]) for d in range(NB - 1)
-    ]
-    for copy in to_states:
-        copy.start()
-
-    total = [tiles[at((x * NZ + NP * b + q) * 8, 8, 8), :] for b in range(NB)]
+
+    total = [tiles[at((3 * NZ + NQ * b + q) * 8, 8, 8), :] for b in range(NB)]
     total = jnp.concatenate(total, axis=0)
-    for k, copy in enumerate(to_near):
-        copy.wait_recv()
+    for k in reversed(range(len(NEAR))):
+        if k == 3:
+            to_cross.start()
+        to_near[k].wait_recv()
         total = total + near_in[pl.ds(k * PIECE, PIECE), :].astype(F32)
     far_own = far_buf.at[at(zb * PIECE, PIECE, 32)]
     far_own[...] = total.astype(BF16)
@@ -209,6 +213,8 @@
     block_pair[0].wait_recv()
     for copy in load_states:
         copy.wait()
+    for copy in dense_pair + block_pair + to_near:
+        copy.wait_send()
     to_cross.wait_recv()
 
     def update_step(i, carry):
@@ -230,7 +236,10 @@
     weight_pair = send(own_weight, own_weight, cross_ss.at[2], cross_rs.at[2], pair)
     weight_pair.start()
 
-    for copy in to_states + to_far:
+    for copy in to_states:
+        copy.wait()
+    to_cross.wait_send()
+    for copy in to_far[::-1]:
         copy.wait_recv()
     dense_sum = jnp.zeros((PIECE, 128), F32)
     for b in range(NB):
@@ -242,50 +251,54 @@
         for i in range(3):
             dnew[pl.ds(b * 24 + 8 * i, 8), :] = new[i]
         news.append(new[0])
-    own_piece = dweights.at[at(c * 512 + mine * PIECE, PIECE, 32)]
+    own_piece = dweights.at[at(c * 512 + (x * NQ + q) * PIECE, PIECE, 32)]
     own_piece[...] = jnp.concatenate(news, axis=0).astype(BF16)
     to_gather = [send(own_piece, own_piece, gather_send.at[k], gather_recv.at[k], near[k]) for k in range(len(NEAR))]
     for copy in to_gather:
         copy.start()
     for i, ref in enumerate((dmaster_out, dmoment_out, dsecond_out)):
         ref[...] = dnew[at(zb * 24 + 8 * i, 8, 8), :]
-
-    weight_cross.wait_recv()
+    for copy in to_far:
+        copy.wait_send()
+
+    weight_cross.wait()
+    weight_pair.wait_send()
     cross_weight = weight_out.at[at((2 * (1 - xh) + c) * ROWS, ROWS, 32)]
     weight_on = send(cross_weight, cross_weight, cross_ss.at[3], cross_rs.at[3], pair)
     weight_on.start()
 
-    def place(core, xx):
-        first = pl.multiple_of(core * 512 + xx * NP * PIECE, 128)
-        for qq in range(NP):
+    def place(core, column, slot):
+        first = pl.multiple_of(core * 512 + column * NQ * PIECE, 128)
+        for qq in range(NQ):
             piece = dweights[pl.ds(pl.multiple_of(first + qq * PIECE, 32), PIECE), :].astype(F32)
             for b in range(NB):
-                spread[pl.ds((NP * b + qq) * 8, 8), :] = piece[b * 8 : (b + 1) * 8]
-        to = at(((xx // 2) * 2 + core) * 32 + (xx % 2) * NZ, NZ, 16)
+                spread[pl.ds((slot * NZ + NQ * b + qq) * 8, 8), :] = piece[b * 8 : (b + 1) * 8]
+        to = dense_rows(column, core)
         for s in range(8):
-            dweight_out[to, s * 128 : (s + 1) * 128] = spread[pl.ds(s, NZ, stride=8), :].astype(BF16)
-
+            row = spread[pl.ds(slot * NZ * 8 + s, NZ, stride=8), :]
+            dweight_out[to, s * 128 : (s + 1) * 128] = row.astype(BF16)
+
+    order = (3, 1, 2, 0)
     backs = []
-    for n, dx in enumerate((0, 1, 3, 2)):
-        for k, (ddx, dq) in enumerate(NEAR):
+    for n in order:
+        dx = (NX - DX[n]) % NX
+        for k, (ddx, dz) in enumerate(NEAR):
             if ddx == dx:
                 to_gather[k].wait_recv()
-        group = dweights.at[at(c * 512 + ((x - dx) % NX) * NP * PIECE, NP * PIECE, 128)]
+        group = dweights.at[at(c * 512 + columns[n] * NQ * PIECE, NQ * PIECE, 128)]
         back = send(group, group, back_send.at[n], back_recv.at[n], pair)
         back.start()
         backs.append(back)
-        place(c, (x - dx) % NX)
-    for n, dx in enumerate((0, 1, 3, 2)):
-        backs[n].wait_recv()
-        place(1 - c, (x - dx) % NX)
-
+        place(c, columns[n], n)
+    for copy in to_gather:
+        copy.wait_send()
     weight_pair.wait_recv()
-    weight_on.wait_recv()
-    for copy in (
-        dense_pair + block_pair + to_near + [to_cross] + to_states + to_far
-        + [weight_cross, weight_pair, weight_on] + to_gather + backs
-    ):
-        copy.wait_send()
+    weight_on.wait()
+    for n, back in zip(order, backs):
+        back.wait_recv()
+        place(1 - c, columns[n], 4 + n)
+    for back in backs:
+        back.wait_send()
 
 
 def store(*refs):
@@ -344,10 +357,10 @@
             pltpu.VMEM((NB * 24, 128), F32),
             pltpu.VMEM((NB * 24, 128), F32),
             pltpu.VMEM((1024, 128), BF16),
-            pltpu.VMEM((128, 128), F32),
-            dma((13,)),
-            dma((4,)),
-            dma((4,)),
+            pltpu.VMEM((1024, 128), F32),
+            dma((15,)),
+            dma((6,)),
+            dma((6,)),
             dma((n,)),
             dma((n,)),
             dma((6,)),
@@ -361,7 +374,7 @@
             pltpu.SemaphoreType.REGULAR,
         ],
         compiler_params=pltpu.CompilerParams(
-            collective_id=0, has_side_effects=True, vmem_limit_bytes=24 * 2**20
+            collective_id=0, has_side_effects=True, vmem_limit_bytes=56 * 2**20
         ),
         name="exchange",
     )(

time: 51.9 us -> 42.2 us (0.81)
  local copies, waits for them, and re-layouts: 6.15 us -> 0 us
  Pallas kernels: 44.7 us -> 41.4 us
    unnamed x18 -> x0, local copies, waits for them, and re-layouts: 6.15 us -> none
    pallas_call x1, Pallas kernels: 43.6 us -> 40.2 us  [shards(): pl.pallas_call(exchange, out_shape=[pltpu.VMEM(s, d) for s, d in shapes],...]
where the time goes in v2:
time: 42.2 us; the launch traced here: 42 us
  Pallas kernels  41.4 us (98%)
  between operations  0.64 us (2%)
    pallas_call x1, Pallas kernels, shards(): pl.pallas_call(exchange, out_shape=[pltpu.VMEM(s, d) for s, d in shapes],...  40.2 us
    pallas_call x1, Pallas kernels, shards(): pl.pallas_call(store, out_shape=[jax.ShapeDtypeStruct(s, d) for s, d in s...  1.16 us

profile of v2, /device:TPU:1, one launch (start us, length us, event | category | flops | bytes accessed | tf_op | source)
XLA Modules:
  0.0 42.0 jit_solution(11877596818909544797)
XLA Ops:
  0.6 40.2 %exchange.1 = (bf16[896,256]{1,0:T(8,128)(2,1)S(1)}, f32[224,256]{1,0:T(8,128)S(1)}, f32[224,256]{1,0:T(8,128)S(1)}, f32[224,256]{1,0:T(8,128)S(1)}, bf16[128,10...) custom-call(bf16[896,256]{1,0:T(8,128)(2,1)} %bitcast.9, ...), custom_call_target="tpu_custom_call" | custom-call | tf_op jit(solution)/shard_map/exchange/pallas_call | solution.py:338
  40.8 1.2 %store.1 = (bf16[896,256]{1,0:T(8,128)(2,1)}, f32[224,256]{1,0:T(8,128)}, f32[224,256]{1,0:T(8,128)}, f32[224,256]{1,0:T(8,128)}, bf16[128,1024]{1,0:T(8,128)(2,...) custom-call(bf16[896,256]{1,0:T(8,128)(2,1)S(1)} %get-tuple-element.24.refs_0_, ...), custom_call_target="tpu_custom_call" | custom-call | tf_op jit(solution)/shard_map/store/pallas_call | solution.py:391

commit v3 on v2

--- a/solution.py
+++ b/solution.py
@@ -27,7 +27,8 @@
 PIECE = NB * 8
 DX = (2, 1, 3, 0)
 DZ = (-2, 1, -1, 0)
-NEAR = [(dx, dz) for dx in DX for dz in DZ if (dx, dz) != (0, 0)]
+GROUPS = ((0,), (1, 2), (3,))
+NEAR = [(DX[n], dz) for group in GROUPS for dz in DZ for n in group if (DX[n], dz) != (0, 0)]
 
 
 def adam_update(weight, moment, second, gradient):
@@ -46,9 +47,9 @@
     partials, counts, master, moment, second, dense, dmaster, dmoment, dsecond,
     weight_out, master_out, moment_out, second_out, dweight_out, dmaster_out, dmoment_out, dsecond_out,
     counts_s, blocks, states, scaled, pair_in, cross_send, cross_in,
-    dense_own, dense_in, tiles, pieces, near_in, far_buf, dstates, dnew, dweights, spread,
+    dense_own, dense_out, dense_in, tiles, pieces, near_in, far_buf, dstates, dnew, dweights, spread,
     load_sem, pair_send, pair_recv, near_send, near_recv, far_send, far_recv,
-    cross_ss, cross_rs, gather_send, gather_recv, back_send, back_recv, known,
+    cross_ss, cross_rs, gather_send, gather_recv, back_send, back_recv, known, pair_in_kernel, all_in_kernel,
 ):
     dp, ex = lax.axis_index("dp"), lax.axis_index("expert")
     xh, c = dp // 2, dp % 2
@@ -67,7 +68,7 @@
     pair = device(x, z, 1 - c)
     cross = device(x + 2, z, c)
     near = [device(x + dx, along(dz), c) for dx, dz in NEAR]
-    near_back = [device(x + NX - dx, along(-dz), c) for dx, dz in NEAR]
+    near_back = [device(x + NX - dx, along(-dz), 1) for dx, dz in NEAR]
     far = [device(x, z + NQ * d, c) for d in range(1, NB)]
 
     def send(src, dst, ss, rs, to):
@@ -96,6 +97,12 @@
         )
         for n, column in enumerate(columns)
     ]
+    load_out = [
+        pltpu.make_async_copy(
+            dense.at[dense_rows(column, 1 - c)], dense_out.at[pl.ds(n * NZ, NZ)], load_sem.at[15 + n]
+        )
+        for n, column in enumerate(columns)
+    ]
     load_dstates = [
         pltpu.make_async_copy(ref, dstates.at[at(zb * 24 + 8 * i, 8, 8)], load_sem.at[9 + i])
         for i, ref in enumerate((dmaster, dmoment, dsecond))
@@ -106,12 +113,43 @@
     ]
 
     barrier = pltpu.get_barrier_semaphore()
-    greeted = near_back + [pair, far[0], far[-1]]
+
+    @pl.when(c == 1)
+    def _():
+        pl.semaphore_signal(barrier, inc=1, device_id=pair, device_id_type=MESH)
+
+    greeted = near_back + [device(x, z + NQ, 1), device(x, z + NZ - NQ, 1)]
     for other in greeted:
         pl.semaphore_signal(barrier, inc=1, device_id=other, device_id_type=MESH)
 
-    load_counts.start()
-    for copy in load_blocks[:2] + load_dense + load_dstates + load_blocks[2:] + load_states:
+    for copy in load_out + load_dense + [load_counts] + load_blocks + load_dstates + load_states:
+        copy.start()
+
+    @pl.when(c == 0)
+    def _():
+        pl.semaphore_wait(barrier, 1)
+        pl.semaphore_signal(pair_in_kernel, inc=1, device_id=pair, device_id_type=MESH)
+
+    @pl.when(c == 1)
+    def _():
+        pl.semaphore_wait(pair_in_kernel, 1)
+
+    dense_pair = [
+        send(
+            dense_out.at[pl.ds(n * NZ, NZ)], dense_in.at[pl.ds(n * NZ, NZ)],
+            pair_send.at[n], pair_recv.at[n], pair,
+        )
+        for n, column in enumerate(columns)
+    ]
+    block_pair = [
+        send(
+            scaled.at[pl.ds(h * ROWS, ROWS)], pair_in.at[pl.ds(h * ROWS, ROWS)],
+            pair_send.at[4 + h], pair_recv.at[4 + h], pair,
+        )
+        for h in range(2)
+    ]
+    for load, copy in zip(load_out, dense_pair):
+        load.wait()
         copy.start()
 
     load_counts.wait()
@@ -126,37 +164,10 @@
         return carry
 
     lax.fori_loop(0, 2 * ROWS // 64, scale_step, 0)
-    for copy in load_dstates:
-        copy.wait()
-
-    pl.semaphore_wait(barrier, len(near) + 3)
-
-    dense_pair = [
-        send(
-            dense.at[dense_rows(column, 1 - c)], dense_in.at[pl.ds(n * NZ, NZ)],
-            pair_send.at[n], pair_recv.at[n], pair,
-        )
-        for n, column in enumerate(columns)
-    ]
-    block_pair = [
-        send(
-            scaled.at[pl.ds(h * ROWS, ROWS)], pair_in.at[pl.ds(h * ROWS, ROWS)],
-            pair_send.at[4 + h], pair_recv.at[4 + h], pair,
-        )
-        for h in range(2)
-    ]
-    for copy in dense_pair + block_pair[::-1]:
-        copy.start()
-    pl.semaphore_signal(known, inc=1, device_id=far[0], device_id_type=MESH)
-    own_states = dstates.at[at(zb * 24, 24, 8)]
-    to_states = [
-        send(own_states, own_states, far_send.at[d], far_recv.at[d], far[d]) for d in range(NB - 1)
-    ]
-    to_states[0].start()
-    to_states[2].start()
-
-    to_near = []
-    for n, dx in enumerate(DX):
+    for copy in block_pair[::-1]:
+        copy.start()
+
+    def sum_column(n):
         load_dense[n].wait()
         dense_pair[n].wait_recv()
         rows = pl.ds(n * NZ, NZ)
@@ -167,18 +178,40 @@
             for half in range(NB // 2):
                 two = [tiles[pl.ds((n * NZ + NQ * (2 * half + k) + qq) * 8, 8), :] for k in range(2)]
                 pieces[pl.ds((n * NQ + qq) * PIECE + half * 16, 16), :] = jnp.concatenate(two, axis=0).astype(BF16)
-        for k, (ddx, dz) in enumerate(NEAR):
-            if ddx == dx:
+
+    for n in range(NX):
+        sum_column(n)
+
+    @pl.when(c == 1)
+    def _():
+        pl.semaphore_wait(barrier, 2 * len(greeted))
+        pl.semaphore_signal(all_in_kernel, inc=1, device_id=pair, device_id_type=MESH)
+
+    @pl.when(c == 0)
+    def _():
+        pl.semaphore_wait(all_in_kernel, 1)
+
+    to_near = []
+    for group in GROUPS:
+        for k, (dx, dz) in enumerate(NEAR):
+            if DX.index(dx) in group:
                 copy = send(
-                    pieces.at[at((n * NQ + along(dz) % NQ) * PIECE, PIECE, 32)],
+                    pieces.at[at((DX.index(dx) * NQ + along(dz) % NQ) * PIECE, PIECE, 32)],
                     near_in.at[pl.ds(k * PIECE, PIECE)],
                     near_send.at[k], near_recv.at[k], near[k],
                 )
                 copy.start()
                 to_near.append(copy)
 
-    pl.semaphore_wait(known, 1)
-    to_states[1].start()
+    pl.semaphore_signal(known, inc=1, device_id=far[0], device_id_type=MESH)
+    for copy in load_dstates:
+        copy.wait()
+    own_states = dstates.at[at(zb * 24, 24, 8)]
+    to_states = [
+        send(own_states, own_states, far_send.at[d], far_recv.at[d], far[d]) for d in range(NB - 1)
+    ]
+    to_states[0].start()
+    to_states[2].start()
 
     load_blocks[2].wait()
     block_pair[1].wait_recv()
@@ -191,6 +224,8 @@
         return carry
 
     lax.fori_loop(0, ROWS // 32, cross_step, 0)
+    pl.semaphore_wait(known, 1)
+    to_states[1].start()
     to_cross = send(cross_send, cross_in, cross_ss.at[0], cross_rs.at[0], cross)
 
     total = [tiles[at((3 * NZ + NQ * b + q) * 8, 8, 8), :] for b in range(NB)]
@@ -350,6 +385,7 @@
             pltpu.VMEM((ROWS, COLS), BF16),
             pltpu.VMEM((64, 1024), BF16),
             pltpu.VMEM((64, 1024), BF16),
+            pltpu.VMEM((64, 1024), BF16),
             pltpu.VMEM((512, 128), F32),
             pltpu.VMEM((512, 128), BF16),
             pltpu.VMEM((n * PIECE, 128), BF16),
@@ -358,7 +394,7 @@
             pltpu.VMEM((NB * 24, 128), F32),
             pltpu.VMEM((1024, 128), BF16),
             pltpu.VMEM((1024, 128), F32),
-            dma((15,)),
+            dma((19,)),
             dma((6,)),
             dma((6,)),
             dma((n,)),
@@ -371,6 +407,8 @@
             dma((n,)),
             dma((4,)),
             dma((4,)),
+            pltpu.SemaphoreType.REGULAR,
+            pltpu.SemaphoreType.REGULAR,
             pltpu.SemaphoreType.REGULAR,
         ],
         compiler_params=pltpu.CompilerParams(

time: 42.2 us -> 41.1 us (0.974)
  Pallas kernels: 41.4 us -> 40.3 us
    pallas_call x1, Pallas kernels: 40.2 us -> 39.2 us  [shards(): pl.pallas_call(exchange, out_shape=[pltpu.VMEM(s, d) for s, d in shapes],...]
where the time goes in v3:
time: 41.1 us; the launch traced here: 41 us
  Pallas kernels  40.3 us (98%)
  between operations  0.64 us (2%)
    pallas_call x1, Pallas kernels, shards(): pl.pallas_call(exchange, out_shape=[pltpu.VMEM(s, d) for s, d in shapes],...  39.2 us
    pallas_call x1, Pallas kernels, shards(): pl.pallas_call(store, out_shape=[jax.ShapeDtypeStruct(s, d) for s, d in s...  1.16 us

profile of v3, /device:TPU:1, one launch (start us, length us, event | category | flops | bytes accessed | tf_op | source)
XLA Modules:
  0.0 41.0 jit_solution(885990804252575219)
XLA Ops:
  0.6 39.2 %exchange.1 = (bf16[896,256]{1,0:T(8,128)(2,1)S(1)}, f32[224,256]{1,0:T(8,128)S(1)}, f32[224,256]{1,0:T(8,128)S(1)}, f32[224,256]{1,0:T(8,128)S(1)}, bf16[128,10...) custom-call(bf16[896,256]{1,0:T(8,128)(2,1)} %bitcast.9, ...), custom_call_target="tpu_custom_call" | custom-call | tf_op jit(solution)/shard_map/exchange/pallas_call | solution.py:373
  39.8 1.2 %store.1 = (bf16[896,256]{1,0:T(8,128)(2,1)}, f32[224,256]{1,0:T(8,128)}, f32[224,256]{1,0:T(8,128)}, f32[224,256]{1,0:T(8,128)}, bf16[128,1024]{1,0:T(8,128)(2,...) custom-call(bf16[896,256]{1,0:T(8,128)(2,1)S(1)} %get-tuple-element.24.refs_0_, ...), custom_call_target="tpu_custom_call" | custom-call | tf_op jit(solution)/shard_map/store/pallas_call | solution.py:429

commit v4 on v3

v4 whole, which is shorter than its diff:
```python
import functools

import jax
import jax.numpy as jnp
from jax import lax
from jax.experimental import pallas as pl
from jax.experimental.pallas import tpu as pltpu
from jax.sharding import PartitionSpec as P

MESH = pl.DeviceIdType.MESH
F32 = jnp.float32
BF16 = jnp.bfloat16

beta_one = 0.9
beta_two = 0.95
epsilon = 1e-08
learn_rate = 0.001
weight_decay = 0.1
bias_one = 1.0 - 0.9**10
bias_two = 1.0 - 0.95**10

NX, NZ, NQ = 4, 16, 4
NB = NZ // NQ
ROWS = 224
COLS = 256
PER_EXPERT = 8
PIECE = NB * 8
NEAR = (
    (1, 2), (3, 2), (0, 3), (0, -3),
    (2, 0), (1, 1), (3, 1), (1, -1), (3, -1), (0, 2), (0, -2),
    (1, 0), (3, 0), (0, 1), (0, -1),
)
FIRST = 4


def adam_update(weight, moment, second, gradient):
    moment_new = beta_one * moment + (1.0 - beta_one) * gradient
    second_new = beta_two * second + (1.0 - beta_two) * gradient * gradient
    ratio = moment_new / bias_one / (jnp.sqrt(second_new / bias_two) + epsilon)
    weight_new = weight - learn_rate * (ratio + weight_decay * weight)
    return (weight_new, moment_new, second_new)


def at(offset, size, unit):
    return pl.ds(pl.multiple_of(offset, unit), size)


def exchange(
    partials, counts, master, moment, second, dense, dmaster, dmoment, dsecond,
    weight_out, master_out, moment_out, second_out, dweight_out, dmaster_out, dmoment_out, dsecond_out,
    counts_s, blocks, states, scaled, pair_in, cross_send, cross_in,
    dense_own, dense_out, dense_in, tiles, pieces, near_in, far_buf, dstates, dnew, dweights, spread,
    load_sem, pair_sem, near_sem, far_sem, cross_sem, gather_sem, back_sem, known, pair_in_kernel, all_in_kernel,
):
    dp, ex = lax.axis_index("dp"), lax.axis_index("expert")
    xh, c = dp // 2, dp % 2
    xl, z = ex // NZ, ex % NZ
    x = 2 * xh + xl
    zb, q = z // NQ, z % NQ
    xc = (x + 2 * zb) % NX
    sign = 1 - 2 * c

    def device(x, z, c):
        return {"dp": ((x % NX) // 2) * 2 + c, "expert": (x % 2) * NZ + z % NZ}

    def slot(xc, q):
        return (xc % 2) * 8 + (xc // 2) * NQ + q

    def class_of(x, z):
        return slot((x + 2 * (z // NQ)) % NX, z % NQ)

    mine = class_of(x, z)

    def along(dz):
        return (z + sign * dz + NZ) % NZ

    pair = device(x, z, 1 - c)
    cross = device(x + 2, z, c)
    near = [device(x + dx, along(dz), c) for dx, dz in NEAR]
    near_back = [device(x + NX - dx, along(-dz), 1) for dx, dz in NEAR]
    far = [device(x + 2 * d, z + NQ * d, c) for d in range(1, NB)]

    def send(src, dst, ss, rs, to):
        return pltpu.make_async_remote_copy(
            src_ref=src, dst_ref=dst, send_sem=ss, recv_sem=rs, device_id=to, device_id_type=MESH
        )

    def wait_for(ref, sem):
        pltpu.make_async_copy(ref, ref, sem).wait()

    def dense_rows(column, core):
        return at(((column // 2) * 2 + core) * 32 + (column % 2) * NZ, NZ, 16)

    def dense_half(core, target, sem):
        return [
            pltpu.make_async_copy(
                dense.at[at((2 * h + core) * 32, 32, 32)], target.at[pl.ds(h * 32, 32)], load_sem.at[sem]
            )
            for h in range(2)
        ]

    own_states = dstates.at[at(zb * 24, 24, 8)]
    loads = dense_half(1 - c, dense_out, 0) + dense_half(c, dense_own, 1)
    loads += [
        pltpu.make_async_copy(counts, counts_s, load_sem.at[2]),
        pltpu.make_async_copy(partials, blocks, load_sem.at[3]),
    ]
    loads += [
        pltpu.make_async_copy(ref, dstates.at[at(zb * 24 + 8 * i, 8, 8)], load_sem.at[4])
        for i, ref in enumerate((dmaster, dmoment, dsecond))
    ]
    loads += [
        pltpu.make_async_copy(ref, states.at[i], load_sem.at[5]) for i, ref in enumerate((master, moment, second))
    ]
    for copy in loads[:2]:
        copy.start()

    barrier = pltpu.get_barrier_semaphore()

    @pl.when(c == 1)
    def _():
        pl.semaphore_signal(barrier, inc=1, device_id=pair, device_id_type=MESH)

    greeted = near_back + [device(x, z + NQ, 1), device(x, z + NZ - NQ, 1)]
    for other in greeted:
        pl.semaphore_signal(barrier, inc=1, device_id=other, device_id_type=MESH)

    for copy in loads[2:]:
        copy.start()

    @pl.when(c == 0)
    def _():
        pl.semaphore_wait(barrier, 1)
        pl.semaphore_signal(pair_in_kernel, inc=1, device_id=pair, device_id_type=MESH)

    @pl.when(c == 1)
    def _():
        pl.semaphore_wait(pair_in_kernel, 1)

    wait_for(dense_out, load_sem.at[0])
    dense_pair = send(dense_out, dense_in, pair_sem.at[0], pair_sem.at[1], pair)
    dense_pair.start()

    loads[4].wait()
    count = counts_s[0, ex // PER_EXPERT].astype(F32)
    inverse = 1.0 / jnp.full((1, COLS), count, F32)
    loads[5].wait()

    def scale(block, start):
        rows = pl.ds(pl.multiple_of(block * ROWS + start, 32), 32)
        return (blocks[rows].astype(F32) * inverse).astype(BF16)

    for h in range(2):
        block = 2 * (xh if h == 0 else 1 - xh) + 1 - c

        def scale_step(i, carry):
            scaled[pl.ds(pl.multiple_of(h * ROWS + i * 32, 32), 32)] = scale(block, i * 32)
            return carry

        lax.fori_loop(0, ROWS // 32, scale_step, 0)
    block_pair = send(scaled, pair_in, pair_sem.at[2], pair_sem.at[3], pair)
    block_pair.start()

    def sum_column(n):
        rows = pl.ds(n * NZ, NZ)
        total = dense_own[rows].astype(F32) + dense_in[rows].astype(F32)
        for s in range(8):
            tiles[pl.ds(n * NZ * 8 + s, NZ, stride=8), :] = total[:, s * 128 : (s + 1) * 128]

    wait_for(dense_own, load_sem.at[1])
    dense_pair.wait_recv()
    for n in range(NX):
        sum_column(n)
    for xx in range(NX):
        for qq in range(NQ):
            for half in range(NB // 2):
                two = [((xx + 2 * b) % NX * NZ + NQ * b + qq) * 8 for b in (2 * half, 2 * half + 1)]
                two = jnp.concatenate([tiles[pl.ds(first, 8), :] for first in two], axis=0)
                pieces[pl.ds(slot(xx, qq) * PIECE + half * 16, 16), :] = two.astype(BF16)

    @pl.when(c == 1)
    def _():
        pl.semaphore_wait(barrier, 2 * len(greeted))
        pl.semaphore_signal(all_in_kernel, inc=1, device_id=pair, device_id_type=MESH)

    @pl.when(c == 0)
    def _():
        pl.semaphore_wait(all_in_kernel, 1)

    to_near = [
        send(
            pieces.at[at(class_of(x + dx, along(dz)) * PIECE, PIECE, 32)],
            near_in.at[pl.ds(k * PIECE, PIECE)],
            near_sem.at[0], near_sem.at[1 if k < FIRST else 2], near[k],
        )
        for k, (dx, dz) in enumerate(NEAR)
    ]
    for copy in to_near:
        copy.start()

    for step in (NQ, NZ - NQ):
        pl.semaphore_signal(known, inc=1, device_id=device(x, z + step, c), device_id_type=MESH)

    block_pair.wait_recv()

    def cross_step(i, carry):
        off = pl.multiple_of(i * 32, 32)
        own = scale(2 * (1 - xh) + c, off)
        other = pair_in[pl.ds(pl.multiple_of(ROWS + off, 32), 32)]
        cross_send[pl.ds(off, 32)] = (own.astype(F32) + other.astype(F32)).astype(BF16)
        return carry

    lax.fori_loop(0, ROWS // 32, cross_step, 0)
    wait_for(own_states, load_sem.at[4])
    pl.semaphore_wait(known, 2)
    to_states = [send(own_states, own_states, far_sem.at[0], far_sem.at[1], far[d]) for d in (1, 0, 2)]
    for copy in to_states:
        copy.start()
    to_cross = send(cross_send, cross_in, cross_sem.at[0], cross_sem.at[1], cross)

    total = [tiles[at(((xc + 2 * b) % NX * NZ + NQ * b + q) * 8, 8, 8), :] for b in range(NB)]
    total = jnp.concatenate(total, axis=0)
    wait_for(near_in.at[pl.ds(FIRST * PIECE, (len(NEAR) - FIRST) * PIECE)], near_sem.at[2])
    to_cross.start()
    for k in range(FIRST, len(NEAR)):
        total = total + near_in[pl.ds(k * PIECE, PIECE), :].astype(F32)
    wait_for(near_in.at[pl.ds(0, FIRST * PIECE)], near_sem.at[1])
    for k in range(FIRST):
        total = total + near_in[pl.ds(k * PIECE, PIECE), :].astype(F32)
    far_own = far_buf.at[at(zb * PIECE, PIECE, 32)]
    far_own[...] = total.astype(BF16)
    to_far = [send(far_own, far_own, far_sem.at[2], far_sem.at[3], far[d]) for d in (1, 0, 2)]
    for copy in to_far:
        copy.start()

    wait_for(states, load_sem.at[5])
    dense_pair.wait_send()
    block_pair.wait_send()
    wait_for(near_in, near_sem.at[0])
    to_cross.wait_recv()

    def update_step(i, carry):
        off = pl.multiple_of(i * 32, 32)
        rows = pl.ds(off, 32)
        own = scale(dp, off)
        gradient = own.astype(F32) + pair_in[rows].astype(F32) + cross_in[rows].astype(F32)
        new, moment_new, second_new = adam_update(states[0, rows], states[1, rows], states[2, rows], gradient)
        master_out[rows] = new
        moment_out[rows] = moment_new
        second_out[rows] = second_new
        weight_out[pl.ds(pl.multiple_of(dp * ROWS + off, 32), 32)] = new.astype(BF16)
        return carry

    lax.fori_loop(0, ROWS // 32, update_step, 0)
    own_weight = weight_out.at[at(dp * ROWS, ROWS, 32)]
    weight_cross = send(own_weight, own_weight, cross_sem.at[2], cross_sem.at[3], cross)
    weight_cross.start()
    weight_pair = send(own_weight, own_weight, cross_sem.at[2], cross_sem.at[4], pair)
    weight_pair.start()

    wait_for(dstates.at[pl.ds(0, 72)], far_sem.at[0])
    wait_for(dstates.at[pl.ds(0, 72)], far_sem.at[1])
    to_cross.wait_send()
    wait_for(far_buf.at[pl.ds(0, 3 * PIECE)], far_sem.at[3])
    dense_sum = jnp.zeros((PIECE, 128), F32)
    for b in range(NB):
        dense_sum = dense_sum + far_buf[pl.ds(b * PIECE, PIECE), :].astype(F32)
    news = []
    for b in range(NB):
        old = [dstates[pl.ds(b * 24 + 8 * i, 8), :] for i in range(3)]
        new = adam_update(*old, dense_sum[b * 8 : (b + 1) * 8])
        for i in range(3):
            dnew[pl.ds(b * 24 + 8 * i, 8), :] = new[i]
        news.append(new[0])
    own_piece = dweights.at[at(c * 512 + mine * PIECE, PIECE, 32)]
    own_piece[...] = jnp.concatenate(news, axis=0).astype(BF16)
    to_gather = [
        send(own_piece, own_piece, gather_sem.at[0], gather_sem.at[1 + xc], other) for other in near
    ]
    for copy in to_gather:
        copy.start()
    for i, ref in enumerate((dmaster_out, dmoment_out, dsecond_out)):
        ref[...] = dnew[at(zb * 24 + 8 * i, 8, 8), :]
    wait_for(far_buf.at[pl.ds(0, 3 * PIECE)], far_sem.at[2])

    weight_cross.wait_recv()
    cross_weight = weight_out.at[at((2 * (1 - xh) + c) * ROWS, ROWS, 32)]
    weight_on = send(cross_weight, cross_weight, cross_sem.at[2], cross_sem.at[4], pair)
    weight_on.start()

    def place(core, parity):
        first = core * 512 + parity * 8 * PIECE
        for qq in range(NQ):
            even = dweights[at(first + qq * PIECE, PIECE, 32), :].astype(F32)
            odd = dweights[at(first + (NQ + qq) * PIECE, PIECE, 32), :].astype(F32)
            for b in range(NB):
                for n, piece in enumerate((even, odd) if b % 2 == 0 else (odd, even)):
                    spread[pl.ds((n * NZ + NQ * b + qq) * 8, 8), :] = piece[b * 8 : (b + 1) * 8]
        for n in range(2):
            to = at((2 * n + core) * 32 + parity * NZ, NZ, 16)
            for s in range(8):
                row = spread[pl.ds(n * NZ * 8 + s, NZ, stride=8), :]
                dweight_out[to, s * 128 : (s + 1) * 128] = row.astype(BF16)

    for step in (0, 2, 1, 3):
        xs = (xc + step) % NX
        pieces_in = NQ - 1 if step == 0 else NQ
        wait_for(dweights.at[pl.ds(0, pieces_in * PIECE)], gather_sem.at[1 + xs])
        group = dweights.at[at(c * 512 + slot(xs, 0) * PIECE, NQ * PIECE, 128)]
        send(group, group, back_sem.at[0], back_sem.at[1 + step % 2], pair).start()
        if step >= 2:
            place(c, (x + step) % 2)
    wait_for(near_in, gather_sem.at[0])
    wait_for(weight_out.at[pl.ds(0, 3 * ROWS)], cross_sem.at[2])
    wait_for(weight_out.at[pl.ds(0, 2 * ROWS)], cross_sem.at[4])
    for step in range(2):
        wait_for(dweights.at[pl.ds(0, 2 * NQ * PIECE)], back_sem.at[1 + step])
        place(1 - c, (x + step) % 2)
    wait_for(dweights.at[pl.ds(0, 4 * NQ * PIECE)], back_sem.at[0])


def store(*refs):
    sources, outs, sem = refs[:8], refs[8:16], refs[16]
    copies = [pltpu.make_async_copy(s, o, sem.at[i]) for i, (s, o) in enumerate(zip(sources, outs))]
    for copy in copies:
        copy.start()
    for copy in copies:
        copy.wait()


def shards(
    expert_partials,
    token_counts,
    expert_master,
    expert_moment,
    expert_second,
    dense_partials,
    dense_master,
    dense_moment,
    dense_second,
):
    hbm = pl.BlockSpec(memory_space=pltpu.HBM)
    vmem = pl.BlockSpec(memory_space=pltpu.VMEM)
    dma = pltpu.SemaphoreType.DMA
    shapes = [
        ((4 * ROWS, COLS), BF16),
        ((ROWS, COLS), F32),
        ((ROWS, COLS), F32),
        ((ROWS, COLS), F32),
        ((128, 1024), BF16),
        ((8, 128), F32),
        ((8, 128), F32),
        ((8, 128), F32),
    ]
    results = pl.pallas_call(
        exchange,
        out_shape=[pltpu.VMEM(s, d) for s, d in shapes],
        in_specs=[hbm] * 9,
        out_specs=[vmem] * 8,
        scratch_shapes=[
            pltpu.SMEM((1, 4), jnp.int32),
            pltpu.VMEM((4 * ROWS, COLS), BF16),
            pltpu.VMEM((3, ROWS, COLS), F32),
            pltpu.VMEM((2 * ROWS, COLS), BF16),
            pltpu.VMEM((2 * ROWS, COLS), BF16),
            pltpu.VMEM((ROWS, COLS), BF16),
            pltpu.VMEM((ROWS, COLS), BF16),
            pltpu.VMEM((64, 1024), BF16),
            pltpu.VMEM((64, 1024), BF16),
            pltpu.VMEM((64, 1024), BF16),
            pltpu.VMEM((512, 128), F32),
            pltpu.VMEM((512, 128), BF16),
            pltpu.VMEM((len(NEAR) * PIECE, 128), BF16),
            pltpu.VMEM((NB * PIECE, 128), BF16),
            pltpu.VMEM((NB * 24, 128), F32),
            pltpu.VMEM((NB * 24, 128), F32),
            pltpu.VMEM((1024, 128), BF16),
            pltpu.VMEM((1024, 128), F32),
            dma((6,)),
            dma((4,)),
            dma((3,)),
            dma((4,)),
            dma((5,)),
            dma((5,)),
            dma((3,)),
            pltpu.SemaphoreType.REGULAR,
            pltpu.SemaphoreType.REGULAR,
            pltpu.SemaphoreType.REGULAR,
        ],
        compiler_params=pltpu.CompilerParams(
            collective_id=0, has_side_effects=True, vmem_limit_bytes=56 * 2**20
        ),
        name="exchange",
    )(
        expert_partials.reshape(4 * ROWS, COLS),
        token_counts,
        expert_master,
        expert_moment,
        expert_second,
        dense_partials.reshape(128, 1024),
        dense_master.reshape(8, 128),
        dense_moment.reshape(8, 128),
        dense_second.reshape(8, 128),
    )
    outs = pl.pallas_call(
        store,
        out_shape=[jax.ShapeDtypeStruct(s, d) for s, d in shapes],
        in_specs=[vmem] * 8,
        out_specs=[hbm] * 8,
        scratch_shapes=[dma((8,))],
        compiler_params=pltpu.CompilerParams(vmem_limit_bytes=8 * 2**20),
        name="store",
    )(*results)
    outs = list(outs)
    outs[4] = outs[4].reshape(128, 1, 1024)
    for i in (5, 6, 7):
        outs[i] = outs[i].reshape(1024)
    return tuple(outs)


def solution(mesh):
    return jax.shard_map(
        shards,
        mesh=mesh,
        in_specs=(
            P("dp", "expert", "tensor"),
            P("dp", None),
            P(("expert", "dp"), "tensor"),
            P(("expert", "dp"), "tensor"),
            P(("expert", "dp"), "tensor"),
            P(("dp", "expert"), None, "tensor", None),
            P(("dp", "expert", "tensor")),
            P(("dp", "expert", "tensor")),
            P(("dp", "expert", "tensor")),
        ),
        out_specs=(
            P("expert", "tensor"),
            P(("expert", "dp"), "tensor"),
            P(("expert", "dp"), "tensor"),
            P(("expert", "dp"), "tensor"),
            P(None, "tensor", None),
            P(("dp", "expert", "tensor")),
            P(("dp", "expert", "tensor")),
            P(("dp", "expert", "tensor")),
        ),
        check_vma=False,
    )
```

time: 41.1 us -> 40.9 us (level)
  no operation moved by 1% of the time
where the time goes in v4:
time: 40.9 us; the launch traced here: 40.8 us
  Pallas kernels  40.1 us (98%)
  between operations  0.64 us (2%)
    pallas_call x1, Pallas kernels, shards(): pl.pallas_call(exchange, out_shape=[pltpu.VMEM(s, d) for s, d in shapes],...  38.9 us
    pallas_call x1, Pallas kernels, shards(): pl.pallas_call(store, out_shape=[jax.ShapeDtypeStruct(s, d) for s, d in s...  1.16 us

profile of v4, /device:TPU:1, one launch (start us, length us, event | category | flops | bytes accessed | tf_op | source)
XLA Modules:
  0.0 40.8 jit_solution(7863955497776212474)
XLA Ops:
  0.6 38.9 %exchange.1 = (bf16[896,256]{1,0:T(8,128)(2,1)S(1)}, f32[224,256]{1,0:T(8,128)S(1)}, f32[224,256]{1,0:T(8,128)S(1)}, f32[224,256]{1,0:T(8,128)S(1)}, bf16[128,10...) custom-call(bf16[896,256]{1,0:T(8,128)(2,1)} %bitcast.9, ...), custom_call_target="tpu_custom_call" | custom-call | tf_op jit(solution)/shard_map/exchange/pallas_call | solution.py:355
  39.6 1.2 %store.1 = (bf16[896,256]{1,0:T(8,128)(2,1)}, f32[224,256]{1,0:T(8,128)}, f32[224,256]{1,0:T(8,128)}, f32[224,256]{1,0:T(8,128)}, bf16[128,1024]{1,0:T(8,128)(2,...) custom-call(bf16[896,256]{1,0:T(8,128)(2,1)S(1)} %get-tuple-element.24.refs_0_, ...), custom_call_target="tpu_custom_call" | custom-call | tf_op jit(solution)/shard_map/store/pallas_call | solution.py:405

commit v5 on v4

--- a/solution.py
+++ b/solution.py
@@ -25,12 +25,11 @@
 COLS = 256
 PER_EXPERT = 8
 PIECE = NB * 8
-NEAR = (
-    (1, 2), (3, 2), (0, 3), (0, -3),
-    (2, 0), (1, 1), (3, 1), (1, -1), (3, -1), (0, 2), (0, -2),
-    (1, 0), (3, 0), (0, 1), (0, -1),
-)
+DX = (2, 1, 3, 0)
+DZ = (-2, 1, -1, 0)
+GROUPS = ((0,), (1, 2), (3,))
 FIRST = 4
+NEAR = [(DX[n], dz) for group in GROUPS for dz in DZ for n in group if (DX[n], dz) != (0, 0)]
 
 
 def adam_update(weight, moment, second, gradient):
@@ -57,19 +56,10 @@
     xl, z = ex // NZ, ex % NZ
     x = 2 * xh + xl
     zb, q = z // NQ, z % NQ
-    xc = (x + 2 * zb) % NX
     sign = 1 - 2 * c
 
     def device(x, z, c):
         return {"dp": ((x % NX) // 2) * 2 + c, "expert": (x % 2) * NZ + z % NZ}
-
-    def slot(xc, q):
-        return (xc % 2) * 8 + (xc // 2) * NQ + q
-
-    def class_of(x, z):
-        return slot((x + 2 * (z // NQ)) % NX, z % NQ)
-
-    mine = class_of(x, z)
 
     def along(dz):
         return (z + sign * dz + NZ) % NZ
@@ -78,7 +68,7 @@
     cross = device(x + 2, z, c)
     near = [device(x + dx, along(dz), c) for dx, dz in NEAR]
     near_back = [device(x + NX - dx, along(-dz), 1) for dx, dz in NEAR]
-    far = [device(x + 2 * d, z + NQ * d, c) for d in range(1, NB)]
+    far = [device(x, z + NQ * d, c) for d in range(1, NB)]
 
     def send(src, dst, ss, rs, to):
         return pltpu.make_async_remote_copy(
@@ -166,17 +156,15 @@
         total = dense_own[rows].astype(F32) + dense_in[rows].astype(F32)
         for s in range(8):
             tiles[pl.ds(n * NZ * 8 + s, NZ, stride=8), :] = total[:, s * 128 : (s + 1) * 128]
+        for qq in range(NQ):
+            for half in range(NB // 2):
+                two = [tiles[pl.ds((n * NZ + NQ * (2 * half + k) + qq) * 8, 8), :] for k in range(2)]
+                pieces[pl.ds((n * NQ + qq) * PIECE + half * 16, 16), :] = jnp.concatenate(two, axis=0).astype(BF16)
 
     wait_for(dense_own, load_sem.at[1])
     dense_pair.wait_recv()
     for n in range(NX):
         sum_column(n)
-    for xx in range(NX):
-        for qq in range(NQ):
-            for half in range(NB // 2):
-                two = [((xx + 2 * b) % NX * NZ + NQ * b + qq) * 8 for b in (2 * half, 2 * half + 1)]
-                two = jnp.concatenate([tiles[pl.ds(first, 8), :] for first in two], axis=0)
-                pieces[pl.ds(slot(xx, qq) * PIECE + half * 16, 16), :] = two.astype(BF16)
 
     @pl.when(c == 1)
     def _():
@@ -189,7 +177,7 @@
 
     to_near = [
         send(
-            pieces.at[at(class_of(x + dx, along(dz)) * PIECE, PIECE, 32)],
+            pieces.at[at(((x + dx) % NX * NQ + along(dz) % NQ) * PIECE, PIECE, 32)],
             near_in.at[pl.ds(k * PIECE, PIECE)],
             near_sem.at[0], near_sem.at[1 if k < FIRST else 2], near[k],
         )
@@ -198,8 +186,11 @@
     for copy in to_near:
         copy.start()
 
-    for step in (NQ, NZ - NQ):
-        pl.semaphore_signal(known, inc=1, device_id=device(x, z + step, c), device_id_type=MESH)
+    pl.semaphore_signal(known, inc=1, device_id=far[0], device_id_type=MESH)
+    wait_for(own_states, load_sem.at[4])
+    to_states = [send(own_states, own_states, far_sem.at[0], far_sem.at[1], far[d]) for d in range(NB - 1)]
+    to_states[0].start()
+    to_states[2].start()
 
     block_pair.wait_recv()
 
@@ -211,14 +202,11 @@
         return carry
 
     lax.fori_loop(0, ROWS // 32, cross_step, 0)
-    wait_for(own_states, load_sem.at[4])
-    pl.semaphore_wait(known, 2)
-    to_states = [send(own_states, own_states, far_sem.at[0], far_sem.at[1], far[d]) for d in (1, 0, 2)]
-    for copy in to_states:
-        copy.start()
+    pl.semaphore_wait(known, 1)
+    to_states[1].start()
     to_cross = send(cross_send, cross_in, cross_sem.at[0], cross_sem.at[1], cross)
 
-    total = [tiles[at(((xc + 2 * b) % NX * NZ + NQ * b + q) * 8, 8, 8), :] for b in range(NB)]
+    total = [tiles[at((x * NZ + NQ * b + q) * 8, 8, 8), :] for b in range(NB)]
     total = jnp.concatenate(total, axis=0)
     wait_for(near_in.at[pl.ds(FIRST * PIECE, (len(NEAR) - FIRST) * PIECE)], near_sem.at[2])
     to_cross.start()
@@ -272,10 +260,11 @@
         for i in range(3):
             dnew[pl.ds(b * 24 + 8 * i, 8), :] = new[i]
         news.append(new[0])
-    own_piece = dweights.at[at(c * 512 + mine * PIECE, PIECE, 32)]
+    own_piece = dweights.at[at(c * 512 + (x * NQ + q) * PIECE, PIECE, 32)]
     own_piece[...] = jnp.concatenate(news, axis=0).astype(BF16)
     to_gather = [
-        send(own_piece, own_piece, gather_sem.at[0], gather_sem.at[1 + xc], other) for other in near
+        send(own_piece, own_piece, gather_sem.at[0], gather_sem.at[1 + dx], near[k])
+        for k, (dx, dz) in enumerate(NEAR)
     ]
     for copy in to_gather:
         copy.start()
@@ -288,34 +277,33 @@
     weight_on = send(cross_weight, cross_weight, cross_sem.at[2], cross_sem.at[4], pair)
     weight_on.start()
 
-    def place(core, parity):
-        first = core * 512 + parity * 8 * PIECE
+    def place(core, column, slot):
+        first = pl.multiple_of(core * 512 + column * NQ * PIECE, 128)
         for qq in range(NQ):
-            even = dweights[at(first + qq * PIECE, PIECE, 32), :].astype(F32)
-            odd = dweights[at(first + (NQ + qq) * PIECE, PIECE, 32), :].astype(F32)
+            piece = dweights[pl.ds(pl.multiple_of(first + qq * PIECE, 32), PIECE), :].astype(F32)
             for b in range(NB):
-                for n, piece in enumerate((even, odd) if b % 2 == 0 else (odd, even)):
-                    spread[pl.ds((n * NZ + NQ * b + qq) * 8, 8), :] = piece[b * 8 : (b + 1) * 8]
-        for n in range(2):
-            to = at((2 * n + core) * 32 + parity * NZ, NZ, 16)
-            for s in range(8):
-                row = spread[pl.ds(n * NZ * 8 + s, NZ, stride=8), :]
-                dweight_out[to, s * 128 : (s + 1) * 128] = row.astype(BF16)
-
-    for step in (0, 2, 1, 3):
-        xs = (xc + step) % NX
-        pieces_in = NQ - 1 if step == 0 else NQ
-        wait_for(dweights.at[pl.ds(0, pieces_in * PIECE)], gather_sem.at[1 + xs])
-        group = dweights.at[at(c * 512 + slot(xs, 0) * PIECE, NQ * PIECE, 128)]
-        send(group, group, back_sem.at[0], back_sem.at[1 + step % 2], pair).start()
-        if step >= 2:
-            place(c, (x + step) % 2)
+                spread[pl.ds((slot * NZ + NQ * b + qq) * 8, 8), :] = piece[b * 8 : (b + 1) * 8]
+        to = dense_rows(column, core)
+        for s in range(8):
+            row = spread[pl.ds(slot * NZ * 8 + s, NZ, stride=8), :]
+            dweight_out[to, s * 128 : (s + 1) * 128] = row.astype(BF16)
+
+    order = (0, 1, 3, 2)
+    for dx in order:
+        column = (x + NX - dx) % NX
+        pieces_in = NQ - 1 if dx == 0 else NQ
+        wait_for(dweights.at[pl.ds(0, pieces_in * PIECE)], gather_sem.at[1 + dx])
+        group = dweights.at[at(c * 512 + column * NQ * PIECE, NQ * PIECE, 128)]
+        send(group, group, back_sem.at[0], back_sem.at[1 if dx != 2 else 2], pair).start()
+        place(c, column, dx)
     wait_for(near_in, gather_sem.at[0])
     wait_for(weight_out.at[pl.ds(0, 3 * ROWS)], cross_sem.at[2])
     wait_for(weight_out.at[pl.ds(0, 2 * ROWS)], cross_sem.at[4])
-    for step in range(2):
-        wait_for(dweights.at[pl.ds(0, 2 * NQ * PIECE)], back_sem.at[1 + step])
-        place(1 - c, (x + step) % 2)
+    wait_for(dweights.at[pl.ds(0, 3 * NQ * PIECE)], back_sem.at[1])
+    for dx in order[:3]:
+        place(1 - c, (x + NX - dx) % NX, 4 + dx)
+    wait_for(dweights.at[pl.ds(0, NQ * PIECE)], back_sem.at[2])
+    place(1 - c, (x + 2) % NX, 6)
     wait_for(dweights.at[pl.ds(0, 4 * NQ * PIECE)], back_sem.at[0])
 
 

time: 40.9 us -> 40.3 us (0.985)
  Pallas kernels: 40.1 us -> 39.5 us
    pallas_call x1, Pallas kernels: 38.9 us -> 38.3 us  [shards(): pl.pallas_call(exchange, out_shape=[pltpu.VMEM(s, d) for s, d in shapes],...]
where the time goes in v5:
time: 40.3 us; the launch traced here: 40.1 us
  Pallas kernels  39.5 us (98%)
  between operations  0.64 us (2%)
    pallas_call x1, Pallas kernels, shards(): pl.pallas_call(exchange, out_shape=[pltpu.VMEM(s, d) for s, d in shapes],...  38.3 us
    pallas_call x1, Pallas kernels, shards(): pl.pallas_call(store, out_shape=[jax.ShapeDtypeStruct(s, d) for s, d in s...  1.16 us

profile of v5, /device:TPU:1, one launch (start us, length us, event | category | flops | bytes accessed | tf_op | source)
XLA Modules:
  0.0 40.1 jit_solution(13132526479895715446)
XLA Ops:
  0.6 38.3 %exchange.1 = (bf16[896,256]{1,0:T(8,128)(2,1)S(1)}, f32[224,256]{1,0:T(8,128)S(1)}, f32[224,256]{1,0:T(8,128)S(1)}, f32[224,256]{1,0:T(8,128)S(1)}, bf16[128,10...) custom-call(bf16[896,256]{1,0:T(8,128)(2,1)} %bitcast.9, ...), custom_call_target="tpu_custom_call" | custom-call | tf_op jit(solution)/shard_map/exchange/pallas_call | solution.py:343
  39.0 1.2 %store.1 = (bf16[896,256]{1,0:T(8,128)(2,1)}, f32[224,256]{1,0:T(8,128)}, f32[224,256]{1,0:T(8,128)}, f32[224,256]{1,0:T(8,128)}, bf16[128,1024]{1,0:T(8,128)(2,...) custom-call(bf16[896,256]{1,0:T(8,128)(2,1)S(1)} %get-tuple-element.24.refs_0_, ...), custom_call_target="tpu_custom_call" | custom-call | tf_op jit(solution)/shard_map/store/pallas_call | solution.py:393

commit v6 on v5

--- a/solution.py
+++ b/solution.py
@@ -56,7 +56,7 @@
     xl, z = ex // NZ, ex % NZ
     x = 2 * xh + xl
     zb, q = z // NQ, z % NQ
-    sign = 1 - 2 * c
+    sign = 2 * c - 1
 
     def device(x, z, c):
         return {"dp": ((x % NX) // 2) * 2 + c, "expert": (x % 2) * NZ + z % NZ}

time: 40.3 us -> 39.7 us (0.985)
  Pallas kernels: 39.5 us -> 38.9 us
    pallas_call x1, Pallas kernels: 38.3 us -> 37.7 us  [shards(): pl.pallas_call(exchange, out_shape=[pltpu.VMEM(s, d) for s, d in shapes],...]
where the time goes in v6:
time: 39.7 us; the launch traced here: 39.5 us
  Pallas kernels  38.9 us (98%)
  between operations  0.64 us (2%)
    pallas_call x1, Pallas kernels, shards(): pl.pallas_call(exchange, out_shape=[pltpu.VMEM(s, d) for s, d in shapes],...  37.7 us
    pallas_call x1, Pallas kernels, shards(): pl.pallas_call(store, out_shape=[jax.ShapeDtypeStruct(s, d) for s, d in s...  1.16 us

profile of v6, /device:TPU:1, one launch (start us, length us, event | category | flops | bytes accessed | tf_op | source)
XLA Modules:
  0.0 39.5 jit_solution(7644348726012087194)
XLA Ops:
  0.6 37.7 %exchange.1 = (bf16[896,256]{1,0:T(8,128)(2,1)S(1)}, f32[224,256]{1,0:T(8,128)S(1)}, f32[224,256]{1,0:T(8,128)S(1)}, f32[224,256]{1,0:T(8,128)S(1)}, bf16[128,10...) custom-call(bf16[896,256]{1,0:T(8,128)(2,1)} %bitcast.9, ...), custom_call_target="tpu_custom_call" | custom-call | tf_op jit(solution)/shard_map/exchange/pallas_call | solution.py:343
  38.4 1.2 %store.1 = (bf16[896,256]{1,0:T(8,128)(2,1)}, f32[224,256]{1,0:T(8,128)}, f32[224,256]{1,0:T(8,128)}, f32[224,256]{1,0:T(8,128)}, bf16[128,1024]{1,0:T(8,128)(2,...) custom-call(bf16[896,256]{1,0:T(8,128)(2,1)S(1)} %get-tuple-element.24.refs_0_, ...), custom_call_target="tpu_custom_call" | custom-call | tf_op jit(solution)/shard_map/store/pallas_call | solution.py:393
